TPU v7x, 32 devices: a whole 2x2x4 slice. The times are simulated.
32 devices in a mesh: row: 16 (over z, x, core), col: 2 (over y).
Axes of the slice: x: 2, y: 2, z: 4, core: 2. Of those that a mesh axis runs over, the one named last changes fastest.
Arguments:
- features: bfloat16 [128, 32768], P(None, 'row'), may hold values from -6 to 6
- weight_in: bfloat16 [128, 512], P(None, 'col'), may hold values from -0.5 to 0.5
- weight_out: bfloat16 [512, 64], replicated, may hold values from -0.25 to 0.25
- score_grad: bfloat16 [64, 32768], P('col', 'row'), may hold values from -0.011962891 to 0.011962891
- band_blocks: bfloat16 [256, 3, 128, 128], P('row'), may hold values from -0.25 to 0.25
- long_blocks: bfloat16 [192, 128, 128], P('row'), may hold values from -0.25 to 0.25
- long_rows: int32 [16, 12], P('row'), may hold values from 0 to 15
- long_sources: int32 [16, 12], replicated, may hold values from 0 to 255, as said below
- long_counts: int32 [16], replicated, may hold values from 1 to 12, as said below
Outputs:
- scores: bfloat16 [64, 32768], P('col', 'row')
- first_grad: float32 [128, 512], P(None, 'col')
- second_grad: float32 [512, 64], P('col')
Inputs may be any that keep to these rules, and one draw needn't show every extreme that they name: `long_sources`: every slot's block column lies on a partition at cycle distance 1 to 3 from the slot's own partition (either direction, indices taken mod the number of partitions); over ALL 12 slots of a partition each of the 6 such partitions is read by exactly 2 slots. Slots s < long_counts[p] are live, the others are ignored; some partition has all 12 live.
All inputs are finite; a program needn't handle non-finite values.
Results may differ from a plain program's by a relative error of at most 0.0065.
Values may be sent and summed in bfloat16 or wider, within the bound.
A program may use at most 128 MiB of HBM per device.

v0:
```python
import jax
import jax.numpy as jnp
from jax import lax
from jax.sharding import PartitionSpec as P

BLK = 128
NB = 16
REACH = 3
SLOTS = 12


def passed_along(x, axis, by):
    devices = lax.axis_size(axis)
    return lax.ppermute(x, axis, [(i, (i + by) % devices) for i in range(devices)])


def signed_offset(owner_part, partition, row_devices):
    offset = jnp.mod(owner_part - partition, row_devices)
    return jnp.where(offset > row_devices // 2, offset - row_devices, offset)


def slot_table(long_sources, long_counts, partition, row_devices):
    source = lax.dynamic_index_in_dim(long_sources, partition, 0, keepdims=False)
    live_count = lax.dynamic_index_in_dim(long_counts, partition, 0, keepdims=False)
    slot_order = jnp.arange(SLOTS, dtype=jnp.int32)
    is_live = slot_order < live_count
    owner_part = source // NB
    local_block = source - owner_part * NB
    offset = signed_offset(owner_part, partition, row_devices)
    same_offset = (
        (offset[:, None] == offset[None, :])
        & is_live[None, :]
        & (slot_order[None, :] < slot_order[:, None])
    )
    slot_rank = jnp.sum(same_offset.astype(jnp.int32), axis=1)
    return (is_live, offset, local_block, slot_rank)


def distances():
    return [distance for distance in range(-REACH, REACH + 1) if distance != 0]


def aggregate(values, band_blocks, long_blocks, row_ids, long_sources, long_counts):
    feature_rows = values.shape[0]
    row_devices = lax.axis_size("row")
    my_index = lax.axis_index("row")
    blocks = values.reshape(feature_rows, NB, BLK)
    is_live, offset, local_block, slot_rank = slot_table(
        long_sources, long_counts, my_index, row_devices
    )
    position = jnp.where(offset < 0, offset + REACH, offset + REACH - 1)
    received = {}
    for distance in distances():
        arrived = passed_along(values, "row", -distance)
        received[distance] = arrived.reshape(feature_rows, NB, BLK)
    panel_pool = jnp.stack([received[distance] for distance in distances()], 0)
    panel_pool = panel_pool.transpose(0, 2, 1, 3).reshape(2 * REACH * NB, feature_rows, BLK)
    slot_index = position * NB + local_block
    before = received[-1][:, NB - 1]
    beyond = received[1][:, 0]
    slot_index = jnp.clip(slot_index, 0, panel_pool.shape[0] - 1)
    panels = jnp.take(panel_pool, slot_index, axis=0)
    contrib = jnp.einsum("kfm,knm->kfn", panels, long_blocks, preferred_element_type=jnp.float32)
    contrib = contrib * is_live.astype(jnp.float32)[:, None, None]
    targets = (
        (row_ids[:, None] == jnp.arange(NB, dtype=jnp.int32)[None, :]) & is_live[:, None]
    ).astype(jnp.float32)
    far_sum = jnp.einsum("kb,kfn->fbn", targets, contrib, precision=lax.Precision.HIGHEST)
    earlier = jnp.concatenate([before[:, None], blocks[:, :-1]], 1)
    onward = jnp.concatenate([blocks[:, 1:], beyond[:, None]], 1)
    near_sum = jnp.einsum(
        "fbm,bnm->fbn", earlier, band_blocks[:, 0], preferred_element_type=jnp.float32
    )
    near_sum = near_sum + jnp.einsum(
        "fbm,bnm->fbn", blocks, band_blocks[:, 1], preferred_element_type=jnp.float32
    )
    near_sum = near_sum + jnp.einsum(
        "fbm,bnm->fbn", onward, band_blocks[:, 2], preferred_element_type=jnp.float32
    )
    return (near_sum + far_sum).reshape(feature_rows, NB * BLK)


def aggregate_back(values, band_blocks, long_blocks, row_ids, long_sources, long_counts):
    feature_rows = values.shape[0]
    row_devices = lax.axis_size("row")
    my_index = lax.axis_index("row")
    blocks = values.reshape(feature_rows, NB, BLK)
    is_live, offset, local_block, slot_rank = slot_table(
        long_sources, long_counts, my_index, row_devices
    )
    to_prior = jnp.einsum(
        "fbn,bnm->fbm", blocks, band_blocks[:, 0], preferred_element_type=jnp.float32
    )
    middle = jnp.einsum(
        "fbn,bnm->fbm", blocks, band_blocks[:, 1], preferred_element_type=jnp.float32
    )
    to_later = jnp.einsum(
        "fbn,bnm->fbm", blocks, band_blocks[:, 2], preferred_element_type=jnp.float32
    )
    zero_block = jnp.zeros((feature_rows, 1, BLK), jnp.float32)
    summed = (
        middle
        + jnp.concatenate([to_prior[:, 1:], zero_block], 1)
        + jnp.concatenate([zero_block, to_later[:, :-1]], 1)
    )
    edge_prior = to_prior[:, 0]
    edge_later = to_later[:, NB - 1]
    gathered_rows = jnp.take(blocks, row_ids, axis=1)
    contrib = jnp.einsum(
        "fkn,knm->kfm", gathered_rows, long_blocks, preferred_element_type=jnp.float32
    )
    contrib = contrib * is_live.astype(jnp.float32)[:, None, None]
    block_hot = local_block[:, None] == jnp.arange(NB, dtype=jnp.int32)[None, :]
    for distance in distances():
        placing = ((is_live & (offset == distance))[:, None] & block_hot).astype(jnp.float32)
        outgoing = jnp.einsum("kb,kfm->fbm", placing, contrib, precision=lax.Precision.HIGHEST)
        if distance == -1:
            outgoing = outgoing.at[:, NB - 1].add(edge_prior)
        if distance == 1:
            outgoing = outgoing.at[:, 0].add(edge_later)
        summed = summed + passed_along(outgoing, "row", distance)
    return summed.reshape(feature_rows, NB * BLK)


def local(
    features,
    weight_in,
    weight_out,
    score_grad,
    band_blocks,
    long_blocks,
    long_rows,
    long_sources,
    long_counts,
):
    row_ids = long_rows[0]
    hidden_count = weight_in.shape[1]
    class_count = score_grad.shape[0]
    col_index = lax.axis_index("col")
    my_rows = lax.dynamic_slice_in_dim(weight_out, col_index * hidden_count, hidden_count, 0)
    hidden_in = jnp.einsum(
        "ih,in->hn", weight_in, features, preferred_element_type=jnp.float32
    ).astype(jnp.bfloat16)
    hidden_sum = aggregate(hidden_in, band_blocks, long_blocks, row_ids, long_sources, long_counts)
    hidden_act = jax.nn.silu(hidden_sum).astype(jnp.bfloat16)
    out_cols = lax.dynamic_slice_in_dim(weight_out, col_index * class_count, class_count, 1)
    class_sum = jnp.einsum(
        "hc,hn->cn",
        out_cols,
        lax.all_gather(hidden_act, "col", axis=0, tiled=True),
        preferred_element_type=jnp.float32,
    )
    class_in = class_sum.astype(jnp.bfloat16)
    scores = aggregate(
        class_in, band_blocks, long_blocks, row_ids, long_sources, long_counts
    ).astype(jnp.bfloat16)
    class_back = aggregate_back(
        score_grad, band_blocks, long_blocks, row_ids, long_sources, long_counts
    ).astype(jnp.bfloat16)
    shard_piece = lax.all_gather(class_back, "col", axis=0, tiled=True)
    hidden_back = jnp.einsum("hc,cn->hn", my_rows, shard_piece, preferred_element_type=jnp.float32)
    block_grad = jnp.einsum(
        "hn,cn->hc", hidden_act, shard_piece, preferred_element_type=jnp.float32
    )
    second_part = block_grad
    hidden_back, second_part = (hidden_back, second_part)
    sigmoid_val = jax.nn.sigmoid(hidden_sum)
    slope_back = (hidden_back * sigmoid_val * (1.0 + hidden_sum * (1.0 - sigmoid_val))).astype(
        jnp.bfloat16
    )
    input_back = aggregate_back(
        slope_back, band_blocks, long_blocks, row_ids, long_sources, long_counts
    ).astype(jnp.bfloat16)
    first_part = jnp.einsum("in,hn->ih", features, input_back, preferred_element_type=jnp.float32)
    first_grad, second_grad = lax.psum((first_part, second_part), "row")
    return (scores, first_grad, second_grad)


def solution(mesh):
    return jax.shard_map(
        local,
        mesh=mesh,
        in_specs=(
            P(None, "row"),
            P(None, "col"),
            P(),
            P("col", "row"),
            P("row", None, None, None),
            P("row", None, None),
            P("row", None),
            P(),
            P(),
        ),
        out_specs=(P("col", "row"), P(None, "col"), P("col", None)),
        check_vma=False,
    )
```

profile of v0, /device:TPU:0, one launch (start us, length us, event | category | flops | bytes accessed | tf_op | source)
XLA Modules:
  0.0 520.7 jit_solution(1792723864568628241)
XLA Ops:
  31.3 4.5 collective-permute-start.14
  36.9 10.6 %collective-permute-start.13 = (f32[32,16,128]{2,0,1:T(8,128)S(1)}, f32[32,16,128]{2,0,1:T(8,128)S(1)}, u32[]{:S(2)}, u32[]{:S(2)}) collective-permute-start(f32[32,16,128]{2,0,1:T(8,128)S(1)} %bitcast.353), channel_id=1, source_target_pairs={{0,28},{2,30},{4,0},{6,2},{8,4},{10,6},{12,8},{14,10},{16,12},{18,... | collective-permute-start | bytes 786440 | tf_op jit(solution)/shard_map/ppermute | solution.py:14
  47.4 4.2 collective-permute-done.16
  54.4 38.9 %collective-permute-done.13 = f32[32,16,128]{2,0,1:T(8,128)S(1)} collective-permute-done((f32[32,16,128]{2,0,1:T(8,128)S(1)}, f32[32,16,128]{2,0,1:T(8,128)S(1)}, u32[]{:S(2)}, u32[]{:S(2)}) %collective-permute-start.13) | collective-permute-done | bytes 262176 | tf_op jit(solution)/shard_map/ppermute | solution.py:14
  102.3 5.9 %all_gather.7 = bf16[64,2048]{1,0:T(8,128)(2,1)} all-gather(bf16[32,2048]{1,0:T(8,128)(2,1)S(1)} %bitcast.345), channel_id=1, replica_groups=mesh['row'=16,'col'=2] {'col'}, dimensions={0}, use_global_device_ids=true | all-gather | bytes 393216 | tf_op jit(solution)/shard_map/all_gather | solution.py:160
  115.9 24.9 %collective-permute-done.4 = bf16[256,2048]{1,0:T(8,128)(2,1)} collective-permute-done((bf16[256,2048]{1,0:T(8,128)(2,1)S(1)}, bf16[256,2048]{1,0:T(8,128)(2,1)}, u32[]{:S(2)}, u32[]{:S(2)}) %collective-permute-start.4) | collective-permute-done | bytes 1048608 | tf_op jit(solution)/shard_map/ppermute | solution.py:14
  142.5 8.6 %collective-permute-done.5 = bf16[256,2048]{1,0:T(8,128)(2,1)} collective-permute-done((bf16[256,2048]{1,0:T(8,128)(2,1)S(1)}, bf16[256,2048]{1,0:T(8,128)(2,1)}, u32[]{:S(2)}, u32[]{:S(2)}) %collective-permute-start.5) | collective-permute-done | bytes 1048608 | tf_op jit(solution)/shard_map/ppermute | solution.py:14
  157.0 3.5 gather_fusion
  161.0 3.6 fusion.22
  164.6 3.2 copy.155
  171.4 3.1 bitcast_add_fusion.1
  184.3 3.6 fusion
  187.9 3.6 fusion.2
  191.5 2.9 copy.212
  194.5 4.2 fusion.4
  198.8 3.0 copy.210
  204.0 3.0 copy.207
  207.0 3.3 copy.330
  215.0 3.6 fusion.6
  218.6 2.9 copy.204
  221.5 3.2 copy.331
  224.7 3.6 fusion.8
  228.3 3.6 fusion.10
  236.4 4.4 collective-permute-start.20
  240.8 2.9 copy.202
  243.8 2.9 copy.200
  252.4 2.9 convolution_convert_fusion.1
  256.9 111.4 %collective-permute-done.22 = f32[256,16,128]{0,2,1:T(8,128)} collective-permute-done((f32[256,16,128]{0,2,1:T(8,128)}, f32[256,16,128]{0,2,1:T(8,128)}, u32[]{:S(2)}, u32[]{:S(2)}) %collective-permute-start.22) | collective-permute-done | bytes 2097184 | tf_op jit(solution)/shard_map/ppermute | solution.py:14
  369.5 10.0 %collective-permute-start.9 = (bf16[32,2048]{1,0:T(8,128)(2,1)}, bf16[32,2048]{1,0:T(8,128)(2,1)}, u32[]{:S(2)}, u32[]{:S(2)}) collective-permute-start(bf16[32,2048]{1,0:T(8,128)(2,1)} %convolution_convert_fusion.1), channel_id=1, source_target_pairs={{0,4},{2,6},{4,8},{6,10},{8,12},{10,14},{12,16},{14,18},{16,20},{1... | collective-permute-start | bytes 393224 | tf_op jit(solution)/shard_map/ppermute | solution.py:14
  379.5 21.2 %collective-permute-done.19 = f32[256,16,128]{0,2,1:T(8,128)} collective-permute-done((f32[256,16,128]{0,2,1:T(8,128)}, f32[256,16,128]{0,2,1:T(8,128)}, u32[]{:S(2)}, u32[]{:S(2)}) %collective-permute-start.19) | collective-permute-done | bytes 2097184 | tf_op jit(solution)/shard_map/ppermute | solution.py:14
  401.6 6.5 %fusion.21 = bf16[256,16,128]{0,2,1:T(8,128)(2,1)S(1)} fusion(f32[256,16,128]{0,2,1:T(8,128)} %collective-permute-done.23, f32[256,16,128]{0,2,1:T(8,128)} %collective-permute-done.22, f32[256,16,128]{0,2,1:T(8,128)} %collective-permute-done.21, f32[256,16,128]{0,2,1:T(8,128)} %collective-permute-done.20, f32[256,16,128]{0,2,1:T(8,128)} %collective-permute-done.19, ...), kind=kOutput, calls=%fused_computation.29 | convolution fusion | flops 138936320 | bytes 19136512 | tf_op jit(solution)/shard_map/fbn,bnm->fbm/dot_general | solution.py:94
  410.9 87.4 %all-reduce.7.cloned.1.call-done = (f32[128,256]{0,1:T(8,128)}, f32[256,64]{0,1:T(8,128)}) async-done(((f32[128,256]{0,1:T(8,128)}, f32[256,64]{0,1:T(8,128)}), (f32[128,256]{0,1:T(8,128)}, f32[256,64]{0,1:T(8,128)})) %all-reduce.7.cloned.1.call-update) | async-done | bytes 196624 | tf_op jit(solution)/shard_map/psum | solution.py:175
  (241 shorter events, 102.6 us)
Async XLA Ops:
  8.0 244.4 %all-gather.2.cloned.1.call-start = ((), (), s32[]{:S(2)}) async-start(), calls=%async_computation | async-start | bytes 3145728 | tf_op jit(solution)/shard_map/all_gather | solution.py:150
  10.3 87.0 %collective-permute-start.2 = (bf16[256,2048]{1,0:T(8,128)(2,1)S(1)}, bf16[256,2048]{1,0:T(8,128)(2,1)}, u32[]{:S(2)}, u32[]{:S(2)}) collective-permute-start(bf16[256,2048]{1,0:T(8,128)(2,1)S(1)} %convolution_convert_fusion), channel_id=1, source_target_pairs={{0,6},{2,8},{4,10},{6,12},{8,14},{10,16},{12,18},{14,20},{16,22},{... | collective-permute-start | bytes 3145736 | tf_op jit(solution)/shard_map/ppermute | solution.py:14
  24.8 12.0 %collective-permute-start.17 = (f32[32,16,128]{2,0,1:T(8,128)S(1)}, f32[32,16,128]{2,0,1:T(8,128)S(1)}, u32[]{:S(2)}, u32[]{:S(2)}) collective-permute-start(f32[32,16,128]{2,0,1:T(8,128)S(1)} %bitcast.351), channel_id=1, source_target_pairs={{0,6},{2,8},{4,10},{6,12},{8,14},{10,16},{12,18},{14,20},{16,22},{... | collective-permute-start | bytes 786440 | tf_op jit(solution)/shard_map/ppermute | solution.py:14
  27.9 23.7 %collective-permute-start.16 = (f32[32,16,128]{2,0,1:T(8,128)S(1)}, f32[32,16,128]{2,0,1:T(8,128)S(1)}, u32[]{:S(2)}, u32[]{:S(2)}) collective-permute-start(f32[32,16,128]{2,0,1:T(8,128)S(1)} %bitcast.350), channel_id=1, source_target_pairs={{0,4},{2,6},{4,8},{6,10},{8,12},{10,14},{12,16},{14,18},{16,20},{1... | collective-permute-start | bytes 786440 | tf_op jit(solution)/shard_map/ppermute | solution.py:14
  30.4 23.9 %collective-permute-start.15 = (f32[32,16,128]{2,0,1:T(8,128)S(1)}, f32[32,16,128]{2,0,1:T(8,128)S(1)}, u32[]{:S(2)}, u32[]{:S(2)}) collective-permute-start(f32[32,16,128]{2,0,1:T(8,128)S(1)} %fusion.110), channel_id=1, source_target_pairs={{0,2},{2,4},{4,6},{6,8},{8,10},{10,12},{12,14},{14,16},{16,18},{18... | collective-permute-start | bytes 786440 | tf_op jit(solution)/shard_map/ppermute | solution.py:14
  30.7 65.5 %copy-start.17 = (f32[32,16,128]{2,0,1:T(8,128)}, f32[32,16,128]{2,0,1:T(8,128)S(1)}, u32[]{:S(2)}) copy-start(f32[32,16,128]{2,0,1:T(8,128)S(1)} %convolution_bitcast_fusion.3) | copy-start | bytes 786436
  31.3 23.0 %collective-permute-start.14 = (f32[32,16,128]{2,0,1:T(8,128)S(1)}, f32[32,16,128]{2,0,1:T(8,128)S(1)}, u32[]{:S(2)}, u32[]{:S(2)}) collective-permute-start(f32[32,16,128]{2,0,1:T(8,128)S(1)} %fusion.111), channel_id=1, source_target_pairs={{0,30},{2,0},{4,2},{6,4},{8,6},{10,8},{12,10},{14,12},{16,14},{18,... | collective-permute-start | bytes 786440 | tf_op jit(solution)/shard_map/ppermute | solution.py:14
  36.9 59.3 %copy-start.20 = (f32[32,16,128]{2,0,1:T(8,128)}, f32[32,16,128]{2,0,1:T(8,128)S(1)}, u32[]{:S(2)}) copy-start(f32[32,16,128]{2,0,1:T(8,128)S(1)} %collective-permute-done.17) | copy-start | bytes 786436
  36.9 56.4 %collective-permute-start.13 = (f32[32,16,128]{2,0,1:T(8,128)S(1)}, f32[32,16,128]{2,0,1:T(8,128)S(1)}, u32[]{:S(2)}, u32[]{:S(2)}) collective-permute-start(f32[32,16,128]{2,0,1:T(8,128)S(1)} %bitcast.353), channel_id=1, source_target_pairs={{0,28},{2,30},{4,0},{6,2},{8,4},{10,6},{12,8},{14,10},{16,12},{18,... | collective-permute-start | bytes 786440 | tf_op jit(solution)/shard_map/ppermute | solution.py:14
  51.6 44.6 %copy-start.22 = (f32[32,16,128]{2,0,1:T(8,128)}, f32[32,16,128]{2,0,1:T(8,128)S(1)}, u32[]{:S(2)}) copy-start(f32[32,16,128]{2,0,1:T(8,128)S(1)} %collective-permute-done.16) | copy-start | bytes 786436
  51.6 44.6 %collective-permute-start.12 = (f32[32,16,128]{2,0,1:T(8,128)S(1)}, f32[32,16,128]{2,0,1:T(8,128)S(1)}, u32[]{:S(2)}, u32[]{:S(2)}) collective-permute-start(f32[32,16,128]{2,0,1:T(8,128)S(1)} %bitcast.352), channel_id=1, source_target_pairs={{0,26},{2,28},{4,30},{6,0},{8,2},{10,4},{12,6},{14,8},{16,10},{18,... | collective-permute-start | bytes 786440 | tf_op jit(solution)/shard_map/ppermute | solution.py:14
  54.3 41.9 %copy-start.24 = (f32[32,16,128]{2,0,1:T(8,128)}, f32[32,16,128]{2,0,1:T(8,128)S(1)}, u32[]{:S(2)}) copy-start(f32[32,16,128]{2,0,1:T(8,128)S(1)} %collective-permute-done.15) | copy-start | bytes 786436
  54.3 55.4 %collective-permute-start.3 = (bf16[256,2048]{1,0:T(8,128)(2,1)S(1)}, bf16[256,2048]{1,0:T(8,128)(2,1)}, u32[]{:S(2)}, u32[]{:S(2)}) collective-permute-start(bf16[256,2048]{1,0:T(8,128)(2,1)S(1)} %convolution_convert_fusion), channel_id=1, source_target_pairs={{0,4},{2,6},{4,8},{6,10},{8,12},{10,14},{12,16},{14,18},{16,20},{1... | collective-permute-start | bytes 3145736 | tf_op jit(solution)/shard_map/ppermute | solution.py:14
  54.3 56.9 %collective-permute-start = (bf16[256,2048]{1,0:T(8,128)(2,1)S(1)}, bf16[256,2048]{1,0:T(8,128)(2,1)}, u32[]{:S(2)}, u32[]{:S(2)}) collective-permute-start(bf16[256,2048]{1,0:T(8,128)(2,1)S(1)} %convolution_convert_fusion), channel_id=1, source_target_pairs={{0,2},{2,4},{4,6},{6,8},{8,10},{10,12},{12,14},{14,16},{16,18},{18... | collective-permute-start | bytes 3145736 | tf_op jit(solution)/shard_map/ppermute | solution.py:14
  93.3 21.1 %collective-permute-start.1 = (bf16[256,2048]{1,0:T(8,128)(2,1)S(1)}, bf16[256,2048]{1,0:T(8,128)(2,1)}, u32[]{:S(2)}, u32[]{:S(2)}) collective-permute-start(bf16[256,2048]{1,0:T(8,128)(2,1)S(1)} %convolution_convert_fusion), channel_id=1, source_target_pairs={{0,30},{2,0},{4,2},{6,4},{8,6},{10,8},{12,10},{14,12},{16,14},{18,... | collective-permute-start | bytes 3145736 | tf_op jit(solution)/shard_map/ppermute | solution.py:14
  96.9 43.9 %collective-permute-start.4 = (bf16[256,2048]{1,0:T(8,128)(2,1)S(1)}, bf16[256,2048]{1,0:T(8,128)(2,1)}, u32[]{:S(2)}, u32[]{:S(2)}) collective-permute-start(bf16[256,2048]{1,0:T(8,128)(2,1)S(1)} %convolution_convert_fusion), channel_id=1, source_target_pairs={{0,28},{2,30},{4,0},{6,2},{8,4},{10,6},{12,8},{14,10},{16,12},{18,... | collective-permute-start | bytes 3145736 | tf_op jit(solution)/shard_map/ppermute | solution.py:14
  97.4 53.8 %collective-permute-start.5 = (bf16[256,2048]{1,0:T(8,128)(2,1)S(1)}, bf16[256,2048]{1,0:T(8,128)(2,1)}, u32[]{:S(2)}, u32[]{:S(2)}) collective-permute-start(bf16[256,2048]{1,0:T(8,128)(2,1)S(1)} %convolution_convert_fusion), channel_id=1, source_target_pairs={{0,26},{2,28},{4,30},{6,0},{8,2},{10,4},{12,6},{14,8},{16,10},{18,... | collective-permute-start | bytes 3145736 | tf_op jit(solution)/shard_map/ppermute | solution.py:14
  194.5 52.2 %collective-permute-start.23 = (f32[256,16,128]{0,2,1:T(8,128)}, f32[256,16,128]{0,2,1:T(8,128)}, u32[]{:S(2)}, u32[]{:S(2)}) collective-permute-start(f32[256,16,128]{0,2,1:T(8,128)} %bitcast.337), channel_id=1, source_target_pairs={{0,6},{2,8},{4,10},{6,12},{8,14},{10,16},{12,18},{14,20},{16,22},{... | collective-permute-start | bytes 6291464 | tf_op jit(solution)/shard_map/ppermute | solution.py:14
  198.7 299.5 %all-reduce.7.cloned.1.call-start = ((), (), s32[]{:S(2)}) async-start(), calls=%async_computation.1 | async-start | bytes 393216 | tf_op jit(solution)/shard_map/psum | solution.py:175
  201.8 166.5 %collective-permute-start.22 = (f32[256,16,128]{0,2,1:T(8,128)}, f32[256,16,128]{0,2,1:T(8,128)}, u32[]{:S(2)}, u32[]{:S(2)}) collective-permute-start(f32[256,16,128]{0,2,1:T(8,128)} %bitcast.334), channel_id=1, source_target_pairs={{0,4},{2,6},{4,8},{6,10},{8,12},{10,14},{12,16},{14,18},{16,20},{1... | collective-permute-start | bytes 6291464 | tf_op jit(solution)/shard_map/ppermute | solution.py:14
  214.8 153.5 %collective-permute-start.21 = (f32[256,16,128]{0,2,1:T(8,128)}, f32[256,16,128]{0,2,1:T(8,128)}, u32[]{:S(2)}, u32[]{:S(2)}) collective-permute-start(f32[256,16,128]{0,2,1:T(8,128)} %fusion.93), channel_id=1, source_target_pairs={{0,2},{2,4},{4,6},{6,8},{8,10},{10,12},{12,14},{14,16},{16,18},{18... | collective-permute-start | bytes 6291464 | tf_op jit(solution)/shard_map/ppermute | solution.py:14
  236.4 133.1 %collective-permute-start.20 = (f32[256,16,128]{0,2,1:T(8,128)}, f32[256,16,128]{0,2,1:T(8,128)}, u32[]{:S(2)}, u32[]{:S(2)}) collective-permute-start(f32[256,16,128]{0,2,1:T(8,128)} %fusion.94), channel_id=1, source_target_pairs={{0,30},{2,0},{4,2},{6,4},{8,6},{10,8},{12,10},{14,12},{16,14},{18,... | collective-permute-start | bytes 6291464 | tf_op jit(solution)/shard_map/ppermute | solution.py:14
  243.8 157.0 %collective-permute-start.19 = (f32[256,16,128]{0,2,1:T(8,128)}, f32[256,16,128]{0,2,1:T(8,128)}, u32[]{:S(2)}, u32[]{:S(2)}) collective-permute-start(f32[256,16,128]{0,2,1:T(8,128)} %bitcast.336), channel_id=1, source_target_pairs={{0,28},{2,30},{4,0},{6,2},{8,4},{10,6},{12,8},{14,10},{16,12},{18,... | collective-permute-start | bytes 6291464 | tf_op jit(solution)/shard_map/ppermute | solution.py:14
  246.6 154.2 %collective-permute-start.18 = (f32[256,16,128]{0,2,1:T(8,128)}, f32[256,16,128]{0,2,1:T(8,128)}, u32[]{:S(2)}, u32[]{:S(2)}) collective-permute-start(f32[256,16,128]{0,2,1:T(8,128)} %bitcast.335), channel_id=1, source_target_pairs={{0,26},{2,28},{4,30},{6,0},{8,2},{10,4},{12,6},{14,8},{16,10},{18,... | collective-permute-start | bytes 6291464 | tf_op jit(solution)/shard_map/ppermute | solution.py:14
  251.3 150.2 %copy-start.2 = (bf16[16,3,128,128]{3,2,1,0:T(8,128)(2,1)S(1)}, bf16[16,3,128,128]{3,2,1,0:T(8,128)(2,1)}, u32[]{:S(2)}) copy-start(bf16[16,3,128,128]{3,2,1,0:T(8,128)(2,1)} %param.21) | copy-start | bytes 4718596
  252.4 149.2 %slice-start = ((f32[256,16,128]{0,2,1:T(8,128)}), f32[256,15,128]{0,2,1:T(8,128)S(1)}, s32[]{:S(2)}) async-start(f32[256,16,128]{0,2,1:T(8,128)} %copy-done.6), calls=%async_computation.2 | async-start | bytes 3932160 | tf_op jit(solution)/shard_map/slice | solution.py:104
  368.3 131.6 %collective-permute-start.6 = (bf16[32,2048]{1,0:T(8,128)(2,1)}, bf16[32,2048]{1,0:T(8,128)(2,1)}, u32[]{:S(2)}, u32[]{:S(2)}) collective-permute-start(bf16[32,2048]{1,0:T(8,128)(2,1)} %convolution_convert_fusion.1), channel_id=1, source_target_pairs={{0,2},{2,4},{4,6},{6,8},{8,10},{10,12},{12,14},{14,16},{16,18},{18... | collective-permute-start | bytes 393224 | tf_op jit(solution)/shard_map/ppermute | solution.py:14
  368.3 132.7 %collective-permute-start.8 = (bf16[32,2048]{1,0:T(8,128)(2,1)}, bf16[32,2048]{1,0:T(8,128)(2,1)}, u32[]{:S(2)}, u32[]{:S(2)}) collective-permute-start(bf16[32,2048]{1,0:T(8,128)(2,1)} %convolution_convert_fusion.1), channel_id=1, source_target_pairs={{0,6},{2,8},{4,10},{6,12},{8,14},{10,16},{12,18},{14,20},{16,22},{... | collective-permute-start | bytes 393224 | tf_op jit(solution)/shard_map/ppermute | solution.py:14
  369.5 132.4 %collective-permute-start.9 = (bf16[32,2048]{1,0:T(8,128)(2,1)}, bf16[32,2048]{1,0:T(8,128)(2,1)}, u32[]{:S(2)}, u32[]{:S(2)}) collective-permute-start(bf16[32,2048]{1,0:T(8,128)(2,1)} %convolution_convert_fusion.1), channel_id=1, source_target_pairs={{0,4},{2,6},{4,8},{6,10},{8,12},{10,14},{12,16},{14,18},{16,20},{1... | collective-permute-start | bytes 393224 | tf_op jit(solution)/shard_map/ppermute | solution.py:14
  400.8 102.0 %collective-permute-start.7 = (bf16[32,2048]{1,0:T(8,128)(2,1)}, bf16[32,2048]{1,0:T(8,128)(2,1)}, u32[]{:S(2)}, u32[]{:S(2)}) collective-permute-start(bf16[32,2048]{1,0:T(8,128)(2,1)} %convolution_convert_fusion.1), channel_id=1, source_target_pairs={{0,30},{2,0},{4,2},{6,4},{8,6},{10,8},{12,10},{14,12},{16,14},{18,... | collective-permute-start | bytes 393224 | tf_op jit(solution)/shard_map/ppermute | solution.py:14
  400.9 104.6 %collective-permute-start.10 = (bf16[32,2048]{1,0:T(8,128)(2,1)}, bf16[32,2048]{1,0:T(8,128)(2,1)}, u32[]{:S(2)}, u32[]{:S(2)}) collective-permute-start(bf16[32,2048]{1,0:T(8,128)(2,1)} %convolution_convert_fusion.1), channel_id=1, source_target_pairs={{0,28},{2,30},{4,0},{6,2},{8,4},{10,6},{12,8},{14,10},{16,12},{18,... | collective-permute-start | bytes 393224 | tf_op jit(solution)/shard_map/ppermute | solution.py:14
  499.9 6.6 %collective-permute-start.11 = (bf16[32,2048]{1,0:T(8,128)(2,1)}, bf16[32,2048]{1,0:T(8,128)(2,1)S(1)}, u32[]{:S(2)}, u32[]{:S(2)}) collective-permute-start(bf16[32,2048]{1,0:T(8,128)(2,1)} %convolution_convert_fusion.1), channel_id=1, source_target_pairs={{0,26},{2,28},{4,30},{6,0},{8,2},{10,4},{12,6},{14,8},{16,10},{18,... | collective-permute-start | bytes 393224 | tf_op jit(solution)/shard_map/ppermute | solution.py:14
  (47 other events, 293.0 us)
Sparse Core Ops, SparseCore 0:
  198.8 35.0 all-gather.1
Sparse Core Ops, SparseCore 1:
  409.3 88.9 all-reduce.6
where the time goes:
time: 529 us; the launch traced here: 521 us
  waiting for transfers between devices  302 us (57%)
  local copies, waits for them, and re-layouts  79.2 us (15%)
  matrix products  61.3 us (12%)
  starting transfers between devices  43.9 us (8%)
  between operations  16.9 us (3%)
  other arithmetic  11.1 us (2%)
  blocking collectives  5.92 us (1%)
    ppermute x24, waiting for transfers between devices, passed_along(): lax.ppermute(x, axis, [(i, (i + by) % devices) for i in range(devices)])  215 us
    psum x1, waiting for transfers between devices, local(): first_grad, second_grad = lax.psum((first_part, second_part), 'row')  87.4 us
    ppermute x24, starting transfers between devices, passed_along(): lax.ppermute(x, axis, [(i, (i + by) % devices) for i in range(devices)])  43.8 us
    unnamed x132, local copies, waits for them, and re-layouts  35 us
    dot_general x12, matrix products, aggregate_back(): jnp.einsum('kb,kfm->fbm', placing, contrib, precision=lax.Precision.HIGHEST)  25.9 us
    dot_general x12, local copies, waits for them, and re-layouts, aggregate_back(): jnp.einsum('kb,kfm->fbm', placing, contrib, precision=lax.Precision.HIGHEST)  18.2 us
  transfers between devices with their start and end apart: 26, of which 11 were waited for; matrix products, arithmetic and copies ran while one was open for 18% of the time, Pallas kernels for 0%

commit v1 on v0

v1 whole, which is shorter than its diff:
```python
import functools

import jax
import jax.numpy as jnp
from jax import lax
from jax.experimental import pallas as pl
from jax.experimental.pallas import tpu as pltpu
from jax.sharding import PartitionSpec as P

BLK = 128
SLOTS = 12
DISTANCES = (-3, -2, -1, 1, 2, 3)
BEFORE = DISTANCES.index(-1)
BEYOND = DISTANCES.index(1)
MESH = pl.DeviceIdType.MESH
F32 = jnp.float32
BF16 = jnp.bfloat16


def nn(a, b):
    return lax.dot_general(a, b, (((1,), (0,)), ((), ())), preferred_element_type=F32)


def nt(a, b):
    return lax.dot_general(a, b, (((1,), (1,)), ((), ())), preferred_element_type=F32)


def lanes(block):
    if isinstance(block, int):
        return pl.ds(block * BLK, BLK)
    return pl.ds(pl.multiple_of(block * BLK, BLK), BLK)


def blocks_sent(pos):
    return 3 if pos in (BEFORE, BEYOND) else 2


def kernel(
    rows_n, cols_n, reduce_here,
    x_ref, win_ref, wout_ref, sg_ref, band_ref, long_ref, rows_ref, src_ref, count_ref,
    scores_ref, first_ref, second_ref,
    xb, sb, xs, xr, gs, gr, cs, cr, zacc, contrib, z, gacc, g2, slope, act, part, part_in, cls, red, red_in, summed,
    x_ss, x_rs, g_ss, g_rs, c_ss, c_rs, gc_ss, gc_rs, p_ss, p_rs, red_ss, red_rs, all_ss, all_rs,
):
    me = lax.axis_index("row")
    mc = lax.axis_index("col")
    nodes = x_ref.shape[1]
    nb = nodes // BLK
    hidden = win_ref.shape[1]
    cc = sg_ref.shape[0]
    wire = gs.dtype

    def row_at(by):
        return lax.rem(me + (by + rows_n), rows_n)

    def col_at(by):
        return lax.rem(mc + by, cols_n)

    barrier = pltpu.get_barrier_semaphore()
    if reduce_here:
        def greet(k, carry):
            pl.semaphore_signal(barrier, inc=1, device_id={"row": row_at(k)}, device_id_type=MESH)
            return carry
        lax.fori_loop(1, rows_n, greet, 0)
        expected = rows_n - 1
    else:
        for d in DISTANCES:
            pl.semaphore_signal(barrier, inc=1, device_id={"row": row_at(d)}, device_id_type=MESH)
        expected = len(DISTANCES)
    for k in range(1, cols_n):
        pl.semaphore_signal(barrier, inc=1, device_id={"col": col_at(k)}, device_id_type=MESH)
    expected += cols_n - 1

    def slots_of(reader, owner):
        low, high = jnp.int32(0), jnp.int32(0)
        for s in range(SLOTS):
            match = (lax.div(src_ref[reader, s], nb) == owner).astype(jnp.int32)
            high = jnp.maximum(high, match * s)
            low = jnp.maximum(low, match * (SLOTS - 1 - s))
        low = SLOTS - 1 - low
        return low, high

    served, read = [], []
    for d in DISTANCES:
        reader = row_at(-d)
        served.append([
            jnp.clip(src_ref[reader, s] - me * nb, 0, nb - 1) for s in slots_of(reader, me)
        ])
        read.append([
            (s, jnp.clip(rows_ref[0, s], 0, nb - 1), (s < count_ref[me]).astype(F32))
            for s in slots_of(me, row_at(d))
        ])

    for r in range(nb):
        xb[r] = x_ref[:, lanes(r)]
        sb[r] = sg_ref[:, lanes(r)].astype(wire)
    for pos in range(6):
        for rank in range(2):
            xs[pos, rank] = xb[served[pos][rank]]
    xs[BEFORE, 2] = xb[nb - 1]
    xs[BEYOND, 2] = xb[0]

    pl.semaphore_wait(barrier, expected)

    def swap(src, dst, ss, rs, pos, to):
        span = pl.ds(0, blocks_sent(pos))
        return pltpu.make_async_remote_copy(
            src_ref=src.at[pos, span], dst_ref=dst.at[pos, span],
            send_sem=ss.at[pos], recv_sem=rs.at[pos],
            device_id={"row": to}, device_id_type=MESH,
        )

    x_copies = [swap(xs, xr, x_ss, x_rs, pos, row_at(-d)) for pos, d in enumerate(DISTANCES)]
    for copy in x_copies:
        copy.start()

    for pos in range(6):
        for rank in range(2):
            s, row, live = read[pos][rank]
            out = nn(sb[row].astype(BF16), long_ref[s])
            gs[pos, rank] = (live * out).astype(wire)
    gs[BEFORE, 2] = nn(sg_ref[:, lanes(0)], band_ref[0, 0]).astype(wire)
    gs[BEYOND, 2] = nn(sg_ref[:, lanes(nb - 1)], band_ref[nb - 1, 2]).astype(wire)
    g_copies = [swap(gs, gr, g_ss, g_rs, pos, row_at(d)) for pos, d in enumerate(DISTANCES)]
    for copy in g_copies:
        copy.start()

    def g_band(r, first, last):
        total = nn(sg_ref[:, lanes(r)], band_ref[r, 1])
        if not last:
            total += nn(sg_ref[:, lanes(r + 1)], band_ref[r + 1, 0])
        if not first:
            total += nn(sg_ref[:, lanes(r - 1)], band_ref[r - 1, 2])
        gacc[r] = total

    def z_band(r, first, last):
        total = nt(x_ref[:, lanes(r)], band_ref[r, 1])
        if not first:
            total += nt(x_ref[:, lanes(r - 1)], band_ref[r, 0])
        if not last:
            total += nt(x_ref[:, lanes(r + 1)], band_ref[r, 2])
        zacc[r] = total

    def both(body):
        body(0, True, False)
        lax.fori_loop(1, nb - 1, lambda r, c: (body(r, False, False), c)[1], 0, unroll=2)
        body(nb - 1, False, True)

    both(g_band)

    for copy in g_copies:
        copy.wait_recv()
    gacc[0] += gr[BEYOND, 2].astype(F32)
    gacc[nb - 1] += gr[BEFORE, 2].astype(F32)

    def g_long(r, carry):
        total = gacc[r]
        for pos in range(6):
            for rank in range(2):
                total += (served[pos][rank] == r).astype(F32) * gr[pos, rank].astype(F32)
        g2[mc, :, lanes(r)] = total.astype(BF16).astype(wire)
        return carry

    lax.fori_loop(0, nb, g_long, 0)

    def g_share(k):
        return pltpu.make_async_remote_copy(
            src_ref=g2.at[mc], dst_ref=g2.at[mc],
            send_sem=gc_ss.at[k - 1], recv_sem=gc_rs.at[k - 1],
            device_id={"col": col_at(k)}, device_id_type=MESH,
        )

    def g_arrives(k):
        return pltpu.make_async_remote_copy(
            src_ref=g2.at[mc], dst_ref=g2.at[col_at(cols_n - k)],
            send_sem=gc_ss.at[k - 1], recv_sem=gc_rs.at[k - 1],
            device_id={"col": col_at(k)}, device_id_type=MESH,
        )

    g_shares = [g_share(k) for k in range(1, cols_n)]
    for copy in g_shares:
        copy.start()

    both(z_band)

    for copy in x_copies:
        copy.wait_recv()
    for pos in range(6):
        for rank in range(2):
            s, row, live = read[pos][rank]
            contrib[2 * pos + rank] = nt(xr[pos, rank], long_ref[s])
    zacc[0] += nt(xr[BEFORE, 2], band_ref[0, 0])
    zacc[nb - 1] += nt(xr[BEYOND, 2], band_ref[nb - 1, 2])

    def z_long(r, carry):
        total = zacc[r]
        for pos in range(6):
            for rank in range(2):
                s, row, live = read[pos][rank]
                total += (live * (row == r).astype(F32)) * contrib[2 * pos + rank]
        z[:, lanes(r)] = total.astype(BF16)
        return carry

    lax.fori_loop(0, nb, z_long, 0)

    win_t = win_ref[...].astype(F32).T.astype(BF16)
    my_out = wout_ref[pl.ds(pl.multiple_of(mc * hidden, hidden), hidden), :]
    out_t = my_out.astype(F32).T.astype(BF16)
    tile = 4 * BLK

    def tile_at(t):
        return pl.ds(pl.multiple_of(t * tile, tile), tile)

    def hidden_tile(t, carry):
        v = nn(win_t, z[:, tile_at(t)])
        sig = 0.5 * jnp.tanh(0.5 * v) + 0.5
        h = (v * sig).astype(BF16)
        act[:, tile_at(t)] = h
        slope[:, tile_at(t)] = sig * (1.0 + v * (1.0 - sig))
        p = nn(out_t, h)
        for c in range(cols_n):
            part[c, :, tile_at(t)] = p[c * cc:(c + 1) * cc]
        return carry

    lax.fori_loop(0, nodes // tile, hidden_tile, 0)

    def p_share(k):
        return pltpu.make_async_remote_copy(
            src_ref=part.at[col_at(k)], dst_ref=part_in.at[k - 1],
            send_sem=p_ss.at[k - 1], recv_sem=p_rs.at[k - 1],
            device_id={"col": col_at(k)}, device_id_type=MESH,
        )

    p_shares = [p_share(k) for k in range(1, cols_n)]
    for copy in p_shares:
        copy.start()

    for k in range(1, cols_n):
        g_arrives(k).wait_recv()

    first_ref[...] = jnp.zeros_like(first_ref)
    second_ref[...] = jnp.zeros_like(second_ref)

    def grad_tile(t, carry):
        g = g2[:, :, tile_at(t)].reshape(cols_n * cc, tile).astype(BF16)
        h = act[:, tile_at(t)]
        second_ref[...] += nt(g, h)
        ds = (nn(my_out, g) * slope[:, tile_at(t)]).astype(BF16)
        first_ref[...] += nt(z[:, tile_at(t)], ds)
        return carry

    lax.fori_loop(0, nodes // tile, grad_tile, 0)

    if reduce_here:
        fr = first_ref.shape[0] // rows_n
        sr = second_ref.shape[0] // rows_n
        for j in range(rows_n):
            red[j, 0:fr] = first_ref[j * fr:(j + 1) * fr]
            red[j, fr:fr + sr] = second_ref[j * sr:(j + 1) * sr]

        def red_copy(k):
            return pltpu.make_async_remote_copy(
                src_ref=red.at[row_at(k)], dst_ref=red_in.at[k - 1],
                send_sem=red_ss.at[k - 1], recv_sem=red_rs.at[k - 1],
                device_id={"row": row_at(k)}, device_id_type=MESH,
            )

        def all_copy(k, slot):
            return pltpu.make_async_remote_copy(
                src_ref=summed.at[me], dst_ref=summed.at[slot],
                send_sem=all_ss.at[k - 1], recv_sem=all_rs.at[k - 1],
                device_id={"row": row_at(k)}, device_id_type=MESH,
            )

        def over_peers(body):
            lax.fori_loop(1, rows_n, lambda k, c: (body(k), c)[1], 0)

        over_peers(lambda k: red_copy(k).start())

    for copy in p_shares:
        copy.wait_recv()

    def class_block(r, carry):
        total = part[mc, :, lanes(r)]
        for k in range(cols_n - 1):
            total += part_in[k, :, lanes(r)]
        cls[r] = total.astype(BF16).astype(wire)
        return carry

    lax.fori_loop(0, nb, class_block, 0, unroll=4)

    for pos in range(6):
        for rank in range(2):
            cs[pos, rank] = cls[served[pos][rank]]
    cs[BEFORE, 2] = cls[nb - 1]
    cs[BEYOND, 2] = cls[0]
    c_copies = [swap(cs, cr, c_ss, c_rs, pos, row_at(-d)) for pos, d in enumerate(DISTANCES)]
    for copy in c_copies:
        copy.start()

    def s_band(r, first, last):
        total = nt(cls[r].astype(BF16), band_ref[r, 1])
        if not first:
            total += nt(cls[r - 1].astype(BF16), band_ref[r, 0])
        if not last:
            total += nt(cls[r + 1].astype(BF16), band_ref[r, 2])
        gacc[r] = total

    both(s_band)

    if reduce_here:
        over_peers(lambda k: red_copy(k).wait_recv())
        total = red[me]
        for k in range(rows_n - 1):
            total += red_in[k]
        summed[me] = total
        over_peers(lambda k: all_copy(k, me).start())

    for copy in c_copies:
        copy.wait_recv()
    for pos in range(6):
        for rank in range(2):
            s, row, live = read[pos][rank]
            contrib[2 * pos + rank, 0:cc] = nt(cr[pos, rank].astype(BF16), long_ref[s])
    gacc[0] += nt(cr[BEFORE, 2].astype(BF16), band_ref[0, 0])
    gacc[nb - 1] += nt(cr[BEYOND, 2].astype(BF16), band_ref[nb - 1, 2])

    def s_long(r, carry):
        total = gacc[r]
        for pos in range(6):
            for rank in range(2):
                s, row, live = read[pos][rank]
                total += (live * (row == r).astype(F32)) * contrib[2 * pos + rank, 0:cc]
        scores_ref[:, lanes(r)] = total.astype(BF16)
        return carry

    lax.fori_loop(0, nb, s_long, 0)

    if reduce_here:
        over_peers(lambda k: all_copy(k, row_at(-k)).wait_recv())
        for j in range(rows_n):
            first_ref[j * fr:(j + 1) * fr] = summed[j, 0:fr]
            second_ref[j * sr:(j + 1) * sr] = summed[j, fr:fr + sr]
        over_peers(lambda k: red_copy(k).wait_send())
        over_peers(lambda k: all_copy(k, me).wait_send())

    for copy in x_copies + g_copies + c_copies + g_shares + p_shares:
        copy.wait_send()


def local(
    features, weight_in, weight_out, score_grad, band_blocks, long_blocks, long_rows, long_sources, long_counts,
):
    rows_n = lax.axis_size("row")
    cols_n = lax.axis_size("col")
    feats, nodes = features.shape
    nb = nodes // BLK
    hidden = weight_in.shape[1]
    cc = score_grad.shape[0]
    classes = weight_out.shape[1]
    wire = BF16 if cc % 16 == 0 else F32
    reduce_here = feats % (8 * rows_n) == 0 and classes % rows_n == 0 and hidden % BLK == 0
    chunk = (feats + classes) // rows_n if reduce_here else 8
    slices = rows_n if reduce_here else 1
    peers = max(slices - 1, 1)
    dma = pltpu.SemaphoreType.DMA
    vmem = pl.BlockSpec(memory_space=pltpu.VMEM)
    smem = pl.BlockSpec(memory_space=pltpu.SMEM)
    scores, first, second = pl.pallas_call(
        functools.partial(kernel, rows_n, cols_n, reduce_here),
        out_shape=(
            jax.ShapeDtypeStruct((cc, nodes), BF16),
            jax.ShapeDtypeStruct((feats, hidden), F32),
            jax.ShapeDtypeStruct((classes, hidden), F32),
        ),
        in_specs=[vmem] * 6 + [smem] * 3,
        out_specs=(vmem, vmem, vmem),
        scratch_shapes=[
            pltpu.VMEM((nb, feats, BLK), BF16),
            pltpu.VMEM((nb, cc, BLK), wire),
            pltpu.VMEM((6, 3, feats, BLK), BF16),
            pltpu.VMEM((6, 3, feats, BLK), BF16),
            pltpu.VMEM((6, 3, cc, BLK), wire),
            pltpu.VMEM((6, 3, cc, BLK), wire),
            pltpu.VMEM((6, 3, cc, BLK), wire),
            pltpu.VMEM((6, 3, cc, BLK), wire),
            pltpu.VMEM((nb, feats, BLK), F32),
            pltpu.VMEM((SLOTS, feats, BLK), F32),
            pltpu.VMEM((feats, nodes), BF16),
            pltpu.VMEM((nb, cc, BLK), F32),
            pltpu.VMEM((cols_n, cc, nodes), wire),
            pltpu.VMEM((hidden, nodes), F32),
            pltpu.VMEM((hidden, nodes), BF16),
            pltpu.VMEM((cols_n, cc, nodes), F32),
            pltpu.VMEM((cols_n - 1, cc, nodes), F32),
            pltpu.VMEM((nb, cc, BLK), wire),
            pltpu.VMEM((slices, chunk, hidden), F32),
            pltpu.VMEM((peers, chunk, hidden), F32),
            pltpu.VMEM((slices, chunk, hidden), F32),
            dma((6,)), dma((6,)), dma((6,)), dma((6,)), dma((6,)), dma((6,)),
            dma((cols_n - 1,)), dma((cols_n - 1,)), dma((cols_n - 1,)), dma((cols_n - 1,)),
            dma((peers,)), dma((peers,)), dma((peers,)), dma((peers,)),
        ],
        compiler_params=pltpu.CompilerParams(
            collective_id=0, has_side_effects=True, vmem_limit_bytes=40 * 1024 * 1024
        ),
    )(features, weight_in, weight_out, score_grad, band_blocks, long_blocks, long_rows, long_sources, long_counts)
    second = second.T
    if not reduce_here:
        first, second = lax.psum((first, second), "row")
    return scores, first, second


def solution(mesh):
    return jax.shard_map(
        local,
        mesh=mesh,
        in_specs=(
            P(None, "row"),
            P(None, "col"),
            P(),
            P("col", "row"),
            P("row", None, None, None),
            P("row", None, None),
            P("row", None),
            P(),
            P(),
        ),
        out_specs=(P("col", "row"), P(None, "col"), P("col", None)),
        check_vma=False,
    )
```

time: 529 us -> 49.8 us (0.09); the launches traced: 521 us -> 48.9 us
  waiting for transfers between devices: 302 us -> 0 us
  local copies, waits for them, and re-layouts: 79.2 us -> 10.1 us
  matrix products: 61.3 us -> 0 us
  starting transfers between devices: 43.9 us -> 0 us
  Pallas kernels: 0 us -> 38.2 us
  between operations: 16.9 us -> 0.66 us
  other arithmetic: 11.1 us -> 0 us
  blocking collectives: 5.92 us -> 0 us
    ppermute x24 -> x0, waiting for transfers between devices: 215 us -> none  [passed_along(): lax.ppermute(x, axis, [(i, (i + by) % devices) for i in range(devices)])]
    psum x1 -> x0, waiting for transfers between devices: 87.4 us -> none  [local(): first_grad, second_grad = lax.psum((first_part, second_part), 'row')]
    dot_general x35 -> x0, matrix products: 61.3 us -> none  [the longest x12 25.9 us: aggregate_back(): jnp.einsum('kb,kfm->fbm', placing, contrib, precision=lax.Precision.HIGHEST)]
    ppermute x24 -> x0, starting transfers between devices: 43.8 us -> none  [passed_along(): lax.ppermute(x, axis, [(i, (i + by) % devices) for i in range(devices)])]
    pallas_call x0 -> x1, Pallas kernels: none -> 38.2 us  [local(): pl.pallas_call(functools.partial(kernel, rows_n, cols_n, reduce_here), ou...]
    unnamed x132 -> x20, local copies, waits for them, and re-layouts: 35 us -> 10.1 us
    dot_general x13 -> x0, local copies, waits for them, and re-layouts: 21.4 us -> none  [the longest x12 18.2 us: aggregate_back(): jnp.einsum('kb,kfm->fbm', placing, contrib, precision=lax.Precision.HIGHEST)]
    gather x4 -> x0, local copies, waits for them, and re-layouts: 8.07 us -> none  [the longest x2 5.19 us: aggregate(): panels = jnp.take(panel_pool, slot_index, axis=0)]
  transfers between devices with their start and end apart: 26 -> 0, of which waited for: 11 -> 0; matrix products, arithmetic and copies ran while one was open for 18% -> 0% of each run, Pallas kernels for 0% -> 0%
where the time goes in v1:
time: 49.8 us; the launch traced here: 48.9 us
  Pallas kernels  38.2 us (77%)
  local copies, waits for them, and re-layouts  10.1 us (20%)
  between operations  0.66 us (1%)
    pallas_call x1, Pallas kernels, local(): pl.pallas_call(functools.partial(kernel, rows_n, cols_n, reduce_here), ou...  38.2 us
    unnamed x20, local copies, waits for them, and re-layouts  10.1 us

profile of v1, /device:TPU:0, one launch (start us, length us, event | category | flops | bytes accessed | tf_op | source)
XLA Modules:
  0.0 48.9 jit_solution(6757116527920806633)
XLA Ops:
  0.6 1.0 %copy.12.wout_ref = bf16[512,64]{1,0:T(8,128)(2,1)S(1)} copy(bf16[512,64]{0,1:T(8,128)(2,1)} %param.11) | data formatting | bytes 131072 | tf_op args[2]
  1.6 0.0 copy-start
  1.6 1.4 %copy-done = bf16[16,3,128,128]{3,2,1,0:T(8,128)(2,1)S(1)} copy-done((bf16[16,3,128,128]{3,2,1,0:T(8,128)(2,1)S(1)}, bf16[16,3,128,128]{3,2,1,0:T(8,128)(2,1)}, u32[]{:S(2)}) %copy-start) | copy-done | bytes 1572888
  3.0 0.0 copy-start.1
  3.0 1.0 %copy-done.1 = bf16[128,2048]{1,0:T(8,128)(2,1)S(1)} copy-done((bf16[128,2048]{1,0:T(8,128)(2,1)S(1)}, bf16[128,2048]{1,0:T(8,128)(2,1)}, u32[]{:S(2)}) %copy-start.1) | copy-done | bytes 524312
  4.0 0.0 copy-start.2
  4.1 1.0 %copy-done.2 = bf16[12,128,128]{2,1,0:T(8,128)(2,1)S(1)} copy-done((bf16[12,128,128]{2,1,0:T(8,128)(2,1)S(1)}, bf16[12,128,128]{2,1,0:T(8,128)(2,1)}, u32[]{:S(2)}) %copy-start.2) | copy-done | bytes 393240
  5.0 0.0 copy-start.3
  5.0 0.9 %copy-done.3 = bf16[32,2048]{1,0:T(8,128)(2,1)S(1)} copy-done((bf16[32,2048]{1,0:T(8,128)(2,1)S(1)}, bf16[32,2048]{1,0:T(8,128)(2,1)}, u32[]{:S(2)}) %copy-start.3) | copy-done | bytes 131096
  5.9 0.0 copy-start.4
  6.0 0.8 %copy-done.4 = bf16[128,256]{1,0:T(8,128)(2,1)S(1)} copy-done((bf16[128,256]{1,0:T(8,128)(2,1)S(1)}, bf16[128,256]{1,0:T(8,128)(2,1)}, u32[]{:S(2)}) %copy-start.4) | copy-done | bytes 65560
  6.8 0.0 copy-start.5
  6.8 0.7 %copy-done.5 = s32[16,12]{1,0:T(8,128)S(1)} copy-done((s32[16,12]{1,0:T(8,128)S(1)}, s32[16,12]{1,0:T(8,128)}, u32[]{:S(2)}) %copy-start.5) | copy-done | bytes 792
  7.5 0.0 copy-start.6
  7.5 0.7 %copy-done.6 = s32[1,12]{1,0:T(1,128)S(1)} copy-done((s32[1,12]{1,0:T(1,128)S(1)}, s32[1,12]{1,0:T(1,128)}, u32[]{:S(2)}) %copy-start.6) | copy-done | bytes 72
  8.1 0.0 copy-start.7
  8.1 0.7 %copy-done.7 = s32[16]{0:T(128)S(1)} copy-done((s32[16]{0:T(128)S(1)}, s32[16]{0:T(128)}, u32[]{:S(2)}) %copy-start.7) | copy-done | bytes 88
  8.8 38.2 %shard_map.112 = (bf16[32,2048]{1,0:T(8,128)(2,1)S(1)}, f32[128,256]{1,0:T(8,128)S(1)}, f32[64,256]{1,0:T(8,128)S(1)}) custom-call(bf16[128,2048]{1,0:T(8,128)(2,1)S(1)} %copy-done.1, bf16[128,256]{1,0:T(8,128)(2,1)S(1)} %copy-done.4, bf16[512,64]{1,0:T(8,128)(2,1)S(1)} %copy.12.wout_ref, bf16[32,2048]{1,0:T(8,128)(2,1)S(1)} %copy-done.3, ...), custom_call_target="tpu_custom_call" | custom-call | tf_op jit(solution)/shard_map/pallas_call | solution.py:369
  47.0 0.7 %copy.16 = bf16[32,2048]{1,0:T(8,128)(2,1)} copy(bf16[32,2048]{1,0:T(8,128)(2,1)S(1)} %get-tuple-element.12) | data formatting | bytes 262144
  47.6 0.7 %copy.17 = f32[128,256]{1,0:T(8,128)} copy(f32[128,256]{1,0:T(8,128)S(1)} %get-tuple-element.13) | data formatting | bytes 262144
  48.3 0.6 %copy.18 = f32[256,64]{0,1:T(8,128)} copy(f32[256,64]{0,1:T(8,128)S(1)} %bitcast.1) | data formatting | bytes 131072
Async XLA Ops:
  1.6 1.4 %copy-start = (bf16[16,3,128,128]{3,2,1,0:T(8,128)(2,1)S(1)}, bf16[16,3,128,128]{3,2,1,0:T(8,128)(2,1)}, u32[]{:S(2)}) copy-start(bf16[16,3,128,128]{3,2,1,0:T(8,128)(2,1)} %band_ref.1) | copy-start | bytes 4718596
  3.0 1.0 %copy-start.1 = (bf16[128,2048]{1,0:T(8,128)(2,1)S(1)}, bf16[128,2048]{1,0:T(8,128)(2,1)}, u32[]{:S(2)}) copy-start(bf16[128,2048]{1,0:T(8,128)(2,1)} %x_ref.1) | copy-start | bytes 1572868
  4.0 1.0 %copy-start.2 = (bf16[12,128,128]{2,1,0:T(8,128)(2,1)S(1)}, bf16[12,128,128]{2,1,0:T(8,128)(2,1)}, u32[]{:S(2)}) copy-start(bf16[12,128,128]{2,1,0:T(8,128)(2,1)} %long_ref.1) | copy-start | bytes 1179652
  5.0 0.9 %copy-start.3 = (bf16[32,2048]{1,0:T(8,128)(2,1)S(1)}, bf16[32,2048]{1,0:T(8,128)(2,1)}, u32[]{:S(2)}) copy-start(bf16[32,2048]{1,0:T(8,128)(2,1)} %sg_ref.1) | copy-start | bytes 393220
  5.9 0.8 %copy-start.4 = (bf16[128,256]{1,0:T(8,128)(2,1)S(1)}, bf16[128,256]{1,0:T(8,128)(2,1)}, u32[]{:S(2)}) copy-start(bf16[128,256]{1,0:T(8,128)(2,1)} %win_ref.1) | copy-start | bytes 196612
  6.8 0.7 %copy-start.5 = (s32[16,12]{1,0:T(8,128)S(1)}, s32[16,12]{1,0:T(8,128)}, u32[]{:S(2)}) copy-start(s32[16,12]{1,0:T(8,128)} %src_ref.1) | copy-start | bytes 2308
  7.5 0.7 %copy-start.6 = (s32[1,12]{1,0:T(1,128)S(1)}, s32[1,12]{1,0:T(1,128)}, u32[]{:S(2)}) copy-start(s32[1,12]{1,0:T(1,128)} %rows_ref.1) | copy-start | bytes 148
  8.1 0.7 %copy-start.7 = (s32[16]{0:T(128)S(1)}, s32[16]{0:T(128)}, u32[]{:S(2)}) copy-start(s32[16]{0:T(128)} %count_ref.1) | copy-start | bytes 196

commit v2 on v1

--- a/solution.py
+++ b/solution.py
@@ -37,9 +37,10 @@
 
 def kernel(
     rows_n, cols_n, reduce_here,
-    x_ref, win_ref, wout_ref, sg_ref, band_ref, long_ref, rows_ref, src_ref, count_ref,
+    x_hbm, win_hbm, wout_hbm, sg_hbm, band_hbm, long_hbm, rows_hbm, src_hbm, count_hbm,
     scores_ref, first_ref, second_ref,
-    xb, sb, xs, xr, gs, gr, cs, cr, zacc, contrib, z, gacc, g2, slope, act, part, part_in, cls, red, red_in, summed,
+    x_ref, win_ref, wout_ref, sg_ref, band_ref, long_ref, rows_ref, src_ref, count_ref, in_sem,
+    xb, sb, xs, xr, gs, gr, cs, cr, zacc, contrib, z, gacc, g2, part, part_out, part_in, cls, red, red_in, summed,
     x_ss, x_rs, g_ss, g_rs, c_ss, c_rs, gc_ss, gc_rs, p_ss, p_rs, red_ss, red_rs, all_ss, all_rs,
 ):
     me = lax.axis_index("row")
@@ -49,6 +50,16 @@
     hidden = win_ref.shape[1]
     cc = sg_ref.shape[0]
     wire = gs.dtype
+
+    operands = [
+        pltpu.make_async_copy(src, dst, in_sem.at[i])
+        for i, (src, dst) in enumerate((
+            (rows_hbm, rows_ref), (src_hbm, src_ref), (count_hbm, count_ref), (sg_hbm, sg_ref), (long_hbm, long_ref),
+            (x_hbm, x_ref), (band_hbm, band_ref), (win_hbm, win_ref), (wout_hbm, wout_ref),
+        ))
+    ]
+    for copy in operands:
+        copy.start()
 
     def row_at(by):
         return lax.rem(me + (by + rows_n), rows_n)
@@ -80,6 +91,8 @@
         low = SLOTS - 1 - low
         return low, high
 
+    for copy in operands[:3]:
+        copy.wait()
     served, read = [], []
     for d in DISTANCES:
         reader = row_at(-d)
@@ -91,9 +104,20 @@
             for s in slots_of(me, row_at(d))
         ])
 
+    for copy in operands[3:5]:
+        copy.wait()
+    for r in range(nb):
+        sb[r] = sg_ref[:, lanes(r)].astype(wire)
+    for pos in range(6):
+        for rank in range(2):
+            s, row, live = read[pos][rank]
+            gs[pos, rank] = (live * nn(sb[row].astype(BF16), long_ref[s])).astype(wire)
+    for copy in operands[5:7]:
+        copy.wait()
+    gs[BEFORE, 2] = nn(sg_ref[:, lanes(0)], band_ref[0, 0]).astype(wire)
+    gs[BEYOND, 2] = nn(sg_ref[:, lanes(nb - 1)], band_ref[nb - 1, 2]).astype(wire)
     for r in range(nb):
         xb[r] = x_ref[:, lanes(r)]
-        sb[r] = sg_ref[:, lanes(r)].astype(wire)
     for pos in range(6):
         for rank in range(2):
             xs[pos, rank] = xb[served[pos][rank]]
@@ -110,43 +134,30 @@
             device_id={"row": to}, device_id_type=MESH,
         )
 
+    g_copies = [swap(gs, gr, g_ss, g_rs, pos, row_at(d)) for pos, d in enumerate(DISTANCES)]
     x_copies = [swap(xs, xr, x_ss, x_rs, pos, row_at(-d)) for pos, d in enumerate(DISTANCES)]
-    for copy in x_copies:
+    for copy in g_copies + x_copies:
         copy.start()
 
-    for pos in range(6):
-        for rank in range(2):
-            s, row, live = read[pos][rank]
-            out = nn(sb[row].astype(BF16), long_ref[s])
-            gs[pos, rank] = (live * out).astype(wire)
-    gs[BEFORE, 2] = nn(sg_ref[:, lanes(0)], band_ref[0, 0]).astype(wire)
-    gs[BEYOND, 2] = nn(sg_ref[:, lanes(nb - 1)], band_ref[nb - 1, 2]).astype(wire)
-    g_copies = [swap(gs, gr, g_ss, g_rs, pos, row_at(d)) for pos, d in enumerate(DISTANCES)]
-    for copy in g_copies:
-        copy.start()
-
-    def g_band(r, first, last):
-        total = nn(sg_ref[:, lanes(r)], band_ref[r, 1])
-        if not last:
-            total += nn(sg_ref[:, lanes(r + 1)], band_ref[r + 1, 0])
-        if not first:
-            total += nn(sg_ref[:, lanes(r - 1)], band_ref[r - 1, 2])
-        gacc[r] = total
-
-    def z_band(r, first, last):
-        total = nt(x_ref[:, lanes(r)], band_ref[r, 1])
-        if not first:
-            total += nt(x_ref[:, lanes(r - 1)], band_ref[r, 0])
-        if not last:
-            total += nt(x_ref[:, lanes(r + 1)], band_ref[r, 2])
-        zacc[r] = total
-
-    def both(body):
-        body(0, True, False)
-        lax.fori_loop(1, nb - 1, lambda r, c: (body(r, False, False), c)[1], 0, unroll=2)
-        body(nb - 1, False, True)
-
-    both(g_band)
+    def three(r):
+        start = (r - 1) * BLK
+        return pl.ds(start if isinstance(r, int) else pl.multiple_of(start, BLK), 3 * BLK)
+
+    def inner(body):
+        lax.fori_loop(1, nb - 1, lambda r, c: (body(r), c)[1], 0, unroll=7)
+
+    def g_band(r):
+        blocks = jnp.concatenate([band_ref[r - 1, 2], band_ref[r, 1], band_ref[r + 1, 0]], 0)
+        gacc[r] = nn(sg_ref[:, three(r)], blocks)
+
+    def z_band(r):
+        blocks = jnp.concatenate([band_ref[r, 0], band_ref[r, 1], band_ref[r, 2]], 1)
+        zacc[r] = nt(x_ref[:, three(r)], blocks)
+
+    last = nb - 1
+    inner(g_band)
+    gacc[0] = nn(sg_ref[:, lanes(0)], band_ref[0, 1]) + nn(sg_ref[:, lanes(1)], band_ref[1, 0])
+    gacc[last] = nn(sg_ref[:, lanes(last)], band_ref[last, 1]) + nn(sg_ref[:, lanes(last - 1)], band_ref[last - 1, 2])
 
     for copy in g_copies:
         copy.wait_recv()
@@ -161,7 +172,7 @@
         g2[mc, :, lanes(r)] = total.astype(BF16).astype(wire)
         return carry
 
-    lax.fori_loop(0, nb, g_long, 0)
+    lax.fori_loop(0, nb, g_long, 0, unroll=4)
 
     def g_share(k):
         return pltpu.make_async_remote_copy(
@@ -181,7 +192,20 @@
     for copy in g_shares:
         copy.start()
 
-    both(z_band)
+    inner(z_band)
+    zacc[0] = nt(xb[0], band_ref[0, 1]) + nt(xb[1], band_ref[0, 2])
+    zacc[last] = nt(xb[last - 1], band_ref[last, 0]) + nt(xb[last], band_ref[last, 1])
+
+    for copy in operands[7:]:
+        copy.wait()
+    win_t = win_ref[...].astype(F32).T.astype(BF16)
+    out_f = jnp.zeros((wout_ref.shape[0], hidden), F32)
+    for c in range(cols_n):
+        out_f += (mc == c).astype(F32) * wout_ref[:, c * hidden:(c + 1) * hidden].astype(F32)
+    out_t = out_f.astype(BF16)
+    my_out = out_f.T.astype(BF16)
+    first_ref[...] = jnp.zeros_like(first_ref)
+    second_ref[...] = jnp.zeros_like(second_ref)
 
     for copy in x_copies:
         copy.wait_recv()
@@ -201,62 +225,48 @@
         z[:, lanes(r)] = total.astype(BF16)
         return carry
 
-    lax.fori_loop(0, nb, z_long, 0)
-
-    win_t = win_ref[...].astype(F32).T.astype(BF16)
-    my_out = wout_ref[pl.ds(pl.multiple_of(mc * hidden, hidden), hidden), :]
-    out_t = my_out.astype(F32).T.astype(BF16)
+    lax.fori_loop(0, nb, z_long, 0, unroll=2)
+
     tile = 4 * BLK
+    tiles = nodes // tile
 
     def tile_at(t):
-        return pl.ds(pl.multiple_of(t * tile, tile), tile)
-
-    def hidden_tile(t, carry):
+        return pl.ds(t * tile, tile)
+
+    def p_share(k, t):
+        return pltpu.make_async_remote_copy(
+            src_ref=part_out.at[col_at(k), :, tile_at(t)], dst_ref=part_in.at[k - 1, :, tile_at(t)],
+            send_sem=p_ss.at[k - 1, t], recv_sem=p_rs.at[k - 1, t],
+            device_id={"col": col_at(k)}, device_id_type=MESH,
+        )
+
+    for k in range(1, cols_n):
+        g_arrives(k).wait_recv()
+    p_shares = []
+    for t in range(tiles):
         v = nn(win_t, z[:, tile_at(t)])
         sig = 0.5 * jnp.tanh(0.5 * v) + 0.5
         h = (v * sig).astype(BF16)
-        act[:, tile_at(t)] = h
-        slope[:, tile_at(t)] = sig * (1.0 + v * (1.0 - sig))
         p = nn(out_t, h)
         for c in range(cols_n):
             part[c, :, tile_at(t)] = p[c * cc:(c + 1) * cc]
-        return carry
-
-    lax.fori_loop(0, nodes // tile, hidden_tile, 0)
-
-    def p_share(k):
-        return pltpu.make_async_remote_copy(
-            src_ref=part.at[col_at(k)], dst_ref=part_in.at[k - 1],
-            send_sem=p_ss.at[k - 1], recv_sem=p_rs.at[k - 1],
-            device_id={"col": col_at(k)}, device_id_type=MESH,
-        )
-
-    p_shares = [p_share(k) for k in range(1, cols_n)]
-    for copy in p_shares:
-        copy.start()
-
-    for k in range(1, cols_n):
-        g_arrives(k).wait_recv()
-
-    first_ref[...] = jnp.zeros_like(first_ref)
-    second_ref[...] = jnp.zeros_like(second_ref)
-
-    def grad_tile(t, carry):
+            part_out[c, :, tile_at(t)] = p[c * cc:(c + 1) * cc].astype(wire)
+        for k in range(1, cols_n):
+            p_shares.append(p_share(k, t))
+            p_shares[-1].start()
         g = g2[:, :, tile_at(t)].reshape(cols_n * cc, tile).astype(BF16)
-        h = act[:, tile_at(t)]
         second_ref[...] += nt(g, h)
-        ds = (nn(my_out, g) * slope[:, tile_at(t)]).astype(BF16)
+        ds = (nn(my_out, g) * (sig * (1.0 + v * (1.0 - sig)))).astype(BF16)
         first_ref[...] += nt(z[:, tile_at(t)], ds)
-        return carry
-
-    lax.fori_loop(0, nodes // tile, grad_tile, 0)
 
     if reduce_here:
         fr = first_ref.shape[0] // rows_n
         sr = second_ref.shape[0] // rows_n
         for j in range(rows_n):
-            red[j, 0:fr] = first_ref[j * fr:(j + 1) * fr]
-            red[j, fr:fr + sr] = second_ref[j * sr:(j + 1) * sr]
+            mine = [first_ref[j * fr:(j + 1) * fr], second_ref[j * sr:(j + 1) * sr]]
+            if red.shape[1] > fr + sr:
+                mine.append(jnp.zeros((red.shape[1] - fr - sr, hidden), F32))
+            red[j] = jnp.concatenate(mine, 0).astype(red.dtype)
 
         def red_copy(k):
             return pltpu.make_async_remote_copy(
@@ -283,7 +293,7 @@
     def class_block(r, carry):
         total = part[mc, :, lanes(r)]
         for k in range(cols_n - 1):
-            total += part_in[k, :, lanes(r)]
+            total += part_in[k, :, lanes(r)].astype(F32)
         cls[r] = total.astype(BF16).astype(wire)
         return carry
 
@@ -298,22 +308,21 @@
     for copy in c_copies:
         copy.start()
 
-    def s_band(r, first, last):
-        total = nt(cls[r].astype(BF16), band_ref[r, 1])
-        if not first:
-            total += nt(cls[r - 1].astype(BF16), band_ref[r, 0])
-        if not last:
-            total += nt(cls[r + 1].astype(BF16), band_ref[r, 2])
-        gacc[r] = total
-
-    both(s_band)
+    def s_band(r):
+        values = jnp.concatenate([cls[r - 1], cls[r], cls[r + 1]], 1).astype(BF16)
+        blocks = jnp.concatenate([band_ref[r, 0], band_ref[r, 1], band_ref[r, 2]], 1)
+        gacc[r] = nt(values, blocks)
+
+    inner(s_band)
+    gacc[0] = nt(cls[0].astype(BF16), band_ref[0, 1]) + nt(cls[1].astype(BF16), band_ref[0, 2])
+    gacc[last] = nt(cls[last - 1].astype(BF16), band_ref[last, 0]) + nt(cls[last].astype(BF16), band_ref[last, 1])
 
     if reduce_here:
         over_peers(lambda k: red_copy(k).wait_recv())
-        total = red[me]
+        total = red[me].astype(F32)
         for k in range(rows_n - 1):
-            total += red_in[k]
-        summed[me] = total
+            total += red_in[k].astype(F32)
+        summed[me] = total.astype(summed.dtype)
         over_peers(lambda k: all_copy(k, me).start())
 
     for copy in c_copies:
@@ -334,13 +343,14 @@
         scores_ref[:, lanes(r)] = total.astype(BF16)
         return carry
 
-    lax.fori_loop(0, nb, s_long, 0)
+    lax.fori_loop(0, nb, s_long, 0, unroll=4)
 
     if reduce_here:
         over_peers(lambda k: all_copy(k, row_at(-k)).wait_recv())
         for j in range(rows_n):
-            first_ref[j * fr:(j + 1) * fr] = summed[j, 0:fr]
-            second_ref[j * sr:(j + 1) * sr] = summed[j, fr:fr + sr]
+            final = summed[j].astype(F32)
+            first_ref[j * fr:(j + 1) * fr] = final[0:fr]
+            second_ref[j * sr:(j + 1) * sr] = final[fr:fr + sr]
         over_peers(lambda k: red_copy(k).wait_send())
         over_peers(lambda k: all_copy(k, me).wait_send())
 
@@ -360,12 +370,11 @@
     classes = weight_out.shape[1]
     wire = BF16 if cc % 16 == 0 else F32
     reduce_here = feats % (8 * rows_n) == 0 and classes % rows_n == 0 and hidden % BLK == 0
-    chunk = (feats + classes) // rows_n if reduce_here else 8
+    chunk = -(-((feats + classes) // rows_n) // 16) * 16 if reduce_here else 16
     slices = rows_n if reduce_here else 1
     peers = max(slices - 1, 1)
     dma = pltpu.SemaphoreType.DMA
     vmem = pl.BlockSpec(memory_space=pltpu.VMEM)
-    smem = pl.BlockSpec(memory_space=pltpu.SMEM)
     scores, first, second = pl.pallas_call(
         functools.partial(kernel, rows_n, cols_n, reduce_here),
         out_shape=(
@@ -373,9 +382,19 @@
             jax.ShapeDtypeStruct((feats, hidden), F32),
             jax.ShapeDtypeStruct((classes, hidden), F32),
         ),
-        in_specs=[vmem] * 6 + [smem] * 3,
+        in_specs=[pl.BlockSpec(memory_space=pl.ANY)] * 9,
         out_specs=(vmem, vmem, vmem),
         scratch_shapes=[
+            pltpu.VMEM(features.shape, BF16),
+            pltpu.VMEM(weight_in.shape, BF16),
+            pltpu.VMEM(weight_out.shape[::-1], BF16),
+            pltpu.VMEM(score_grad.shape, BF16),
+            pltpu.VMEM(band_blocks.shape, BF16),
+            pltpu.VMEM(long_blocks.shape, BF16),
+            pltpu.SMEM(long_rows.shape, jnp.int32),
+            pltpu.SMEM(long_sources.shape, jnp.int32),
+            pltpu.SMEM(long_counts.shape, jnp.int32),
+            dma((9,)),
             pltpu.VMEM((nb, feats, BLK), BF16),
             pltpu.VMEM((nb, cc, BLK), wire),
             pltpu.VMEM((6, 3, feats, BLK), BF16),
@@ -389,22 +408,21 @@
             pltpu.VMEM((feats, nodes), BF16),
             pltpu.VMEM((nb, cc, BLK), F32),
             pltpu.VMEM((cols_n, cc, nodes), wire),
-            pltpu.VMEM((hidden, nodes), F32),
-            pltpu.VMEM((hidden, nodes), BF16),
             pltpu.VMEM((cols_n, cc, nodes), F32),
-            pltpu.VMEM((cols_n - 1, cc, nodes), F32),
+            pltpu.VMEM((cols_n, cc, nodes), wire),
+            pltpu.VMEM((cols_n - 1, cc, nodes), wire),
             pltpu.VMEM((nb, cc, BLK), wire),
-            pltpu.VMEM((slices, chunk, hidden), F32),
-            pltpu.VMEM((peers, chunk, hidden), F32),
-            pltpu.VMEM((slices, chunk, hidden), F32),
+            pltpu.VMEM((slices, chunk, hidden), BF16),
+            pltpu.VMEM((peers, chunk, hidden), BF16),
+            pltpu.VMEM((slices, chunk, hidden), BF16),
             dma((6,)), dma((6,)), dma((6,)), dma((6,)), dma((6,)), dma((6,)),
-            dma((cols_n - 1,)), dma((cols_n - 1,)), dma((cols_n - 1,)), dma((cols_n - 1,)),
+            dma((cols_n - 1,)), dma((cols_n - 1,)), dma((cols_n - 1, nodes // (4 * BLK))), dma((cols_n - 1, nodes // (4 * BLK))),
             dma((peers,)), dma((peers,)), dma((peers,)), dma((peers,)),
         ],
         compiler_params=pltpu.CompilerParams(
             collective_id=0, has_side_effects=True, vmem_limit_bytes=40 * 1024 * 1024
         ),
-    )(features, weight_in, weight_out, score_grad, band_blocks, long_blocks, long_rows, long_sources, long_counts)
+    )(features, weight_in, weight_out.T, score_grad, band_blocks, long_blocks, long_rows, long_sources, long_counts)
     second = second.T
     if not reduce_here:
         first, second = lax.psum((first, second), "row")

time: 49.8 us -> 42 us (0.84)
  Pallas kernels: 38.2 us -> 31 us
    pallas_call x1, Pallas kernels: 38.2 us -> 31 us  [local(): pl.pallas_call(functools.partial(kernel, rows_n, cols_n, reduce_here), ou...]
    unnamed x20 -> x21, local copies, waits for them, and re-layouts: 10.1 us -> 9.97 us
where the time goes in v2:
time: 42 us; the launch traced here: 41.6 us
  Pallas kernels  31 us (74%)
  local copies, waits for them, and re-layouts  9.97 us (24%)
  between operations  0.66 us (2%)
    pallas_call x1, Pallas kernels, local(): pl.pallas_call(functools.partial(kernel, rows_n, cols_n, reduce_here), ou...  31 us
    unnamed x21, local copies, waits for them, and re-layouts  9.97 us

profile of v2, /device:TPU:0, one launch (start us, length us, event | category | flops | bytes accessed | tf_op | source)
XLA Modules:
  0.0 41.6 jit_solution(305489618084396945)
XLA Ops:
  0.6 0.0 copy-start
  0.6 1.4 %copy-done = bf16[16,3,128,128]{3,2,1,0:T(8,128)(2,1)S(1)} copy-done((bf16[16,3,128,128]{3,2,1,0:T(8,128)(2,1)S(1)}, bf16[16,3,128,128]{3,2,1,0:T(8,128)(2,1)}, u32[]{:S(2)}) %copy-start) | copy-done | bytes 1572888
  2.0 0.0 copy-start.1
  2.0 1.0 %copy-done.1 = bf16[128,2048]{1,0:T(8,128)(2,1)S(1)} copy-done((bf16[128,2048]{1,0:T(8,128)(2,1)S(1)}, bf16[128,2048]{1,0:T(8,128)(2,1)}, u32[]{:S(2)}) %copy-start.1) | copy-done | bytes 524312
  3.1 0.0 copy-start.2
  3.1 1.0 %copy-done.2 = bf16[12,128,128]{2,1,0:T(8,128)(2,1)S(1)} copy-done((bf16[12,128,128]{2,1,0:T(8,128)(2,1)S(1)}, bf16[12,128,128]{2,1,0:T(8,128)(2,1)}, u32[]{:S(2)}) %copy-start.2) | copy-done | bytes 393240
  4.1 0.0 copy-start.3
  4.1 0.9 %copy-done.3 = bf16[32,2048]{1,0:T(8,128)(2,1)S(1)} copy-done((bf16[32,2048]{1,0:T(8,128)(2,1)S(1)}, bf16[32,2048]{1,0:T(8,128)(2,1)}, u32[]{:S(2)}) %copy-start.3) | copy-done | bytes 131096
  5.0 0.0 copy-start.4
  5.0 0.8 %copy-done.4 = bf16[128,256]{1,0:T(8,128)(2,1)S(1)} copy-done((bf16[128,256]{1,0:T(8,128)(2,1)S(1)}, bf16[128,256]{1,0:T(8,128)(2,1)}, u32[]{:S(2)}) %copy-start.4) | copy-done | bytes 65560
  5.8 0.0 copy-start.5
  5.8 0.8 %copy-done.5 = bf16[512,64]{0,1:T(8,128)(2,1)S(1)} copy-done((bf16[512,64]{0,1:T(8,128)(2,1)S(1)}, bf16[512,64]{0,1:T(8,128)(2,1)}, u32[]{:S(2)}) %copy-start.5) | copy-done | bytes 65560
  6.7 0.0 copy-start.6
  6.7 0.7 %copy-done.6 = s32[16,12]{1,0:T(8,128)S(1)} copy-done((s32[16,12]{1,0:T(8,128)S(1)}, s32[16,12]{1,0:T(8,128)}, u32[]{:S(2)}) %copy-start.6) | copy-done | bytes 792
  7.4 0.0 copy-start.7
  7.4 0.7 %copy-done.7 = s32[1,12]{1,0:T(1,128)S(1)} copy-done((s32[1,12]{1,0:T(1,128)S(1)}, s32[1,12]{1,0:T(1,128)}, u32[]{:S(2)}) %copy-start.7) | copy-done | bytes 72
  8.0 0.0 copy-start.8
  8.0 0.7 %copy-done.8 = s32[16]{0:T(128)S(1)} copy-done((s32[16]{0:T(128)S(1)}, s32[16]{0:T(128)}, u32[]{:S(2)}) %copy-start.8) | copy-done | bytes 88
  8.7 31.0 %shard_map.112 = (bf16[32,2048]{1,0:T(8,128)(2,1)S(1)}, f32[128,256]{1,0:T(8,128)S(1)}, f32[64,256]{1,0:T(8,128)S(1)}) custom-call(bf16[128,2048]{1,0:T(8,128)(2,1)S(1)} %copy-done.1, bf16[128,256]{1,0:T(8,128)(2,1)S(1)} %copy-done.4, bf16[64,512]{1,0:T(8,128)(2,1)S(1)} %bitcast.2, bf16[32,2048]{1,0:T(8,128)(2,1)S(1)} %copy-done.3, ...), custom_call_target="tpu_custom_call" | custom-call | tf_op jit(solution)/shard_map/pallas_call | solution.py:378
  39.7 0.7 %copy.15 = bf16[32,2048]{1,0:T(8,128)(2,1)} copy(bf16[32,2048]{1,0:T(8,128)(2,1)S(1)} %get-tuple-element.12) | data formatting | bytes 262144
  40.3 0.7 %copy.16 = f32[128,256]{1,0:T(8,128)} copy(f32[128,256]{1,0:T(8,128)S(1)} %get-tuple-element.13) | data formatting | bytes 262144
  41.0 0.6 %copy.17 = f32[256,64]{0,1:T(8,128)} copy(f32[256,64]{0,1:T(8,128)S(1)} %bitcast.3) | data formatting | bytes 131072
Async XLA Ops:
  0.6 1.4 %copy-start = (bf16[16,3,128,128]{3,2,1,0:T(8,128)(2,1)S(1)}, bf16[16,3,128,128]{3,2,1,0:T(8,128)(2,1)}, u32[]{:S(2)}) copy-start(bf16[16,3,128,128]{3,2,1,0:T(8,128)(2,1)} %band_hbm.1) | copy-start | bytes 4718596
  2.0 1.0 %copy-start.1 = (bf16[128,2048]{1,0:T(8,128)(2,1)S(1)}, bf16[128,2048]{1,0:T(8,128)(2,1)}, u32[]{:S(2)}) copy-start(bf16[128,2048]{1,0:T(8,128)(2,1)} %x_hbm.1) | copy-start | bytes 1572868
  3.1 1.0 %copy-start.2 = (bf16[12,128,128]{2,1,0:T(8,128)(2,1)S(1)}, bf16[12,128,128]{2,1,0:T(8,128)(2,1)}, u32[]{:S(2)}) copy-start(bf16[12,128,128]{2,1,0:T(8,128)(2,1)} %long_hbm.1) | copy-start | bytes 1179652
  4.1 0.9 %copy-start.3 = (bf16[32,2048]{1,0:T(8,128)(2,1)S(1)}, bf16[32,2048]{1,0:T(8,128)(2,1)}, u32[]{:S(2)}) copy-start(bf16[32,2048]{1,0:T(8,128)(2,1)} %sg_hbm.1) | copy-start | bytes 393220
  5.0 0.8 %copy-start.4 = (bf16[128,256]{1,0:T(8,128)(2,1)S(1)}, bf16[128,256]{1,0:T(8,128)(2,1)}, u32[]{:S(2)}) copy-start(bf16[128,256]{1,0:T(8,128)(2,1)} %win_hbm.1) | copy-start | bytes 196612
  5.8 0.8 %copy-start.5 = (bf16[512,64]{0,1:T(8,128)(2,1)S(1)}, bf16[512,64]{0,1:T(8,128)(2,1)}, u32[]{:S(2)}) copy-start(bf16[512,64]{0,1:T(8,128)(2,1)} %param.11) | copy-start | bytes 196612
  6.7 0.7 %copy-start.6 = (s32[16,12]{1,0:T(8,128)S(1)}, s32[16,12]{1,0:T(8,128)}, u32[]{:S(2)}) copy-start(s32[16,12]{1,0:T(8,128)} %src_hbm.1) | copy-start | bytes 2308
  7.4 0.7 %copy-start.7 = (s32[1,12]{1,0:T(1,128)S(1)}, s32[1,12]{1,0:T(1,128)}, u32[]{:S(2)}) copy-start(s32[1,12]{1,0:T(1,128)} %rows_hbm.1) | copy-start | bytes 148
  8.0 0.7 %copy-start.8 = (s32[16]{0:T(128)S(1)}, s32[16]{0:T(128)}, u32[]{:S(2)}) copy-start(s32[16]{0:T(128)} %count_hbm.1) | copy-start | bytes 196

commit v3 on v2

--- a/solution.py
+++ b/solution.py
@@ -12,6 +12,7 @@
 DISTANCES = (-3, -2, -1, 1, 2, 3)
 BEFORE = DISTANCES.index(-1)
 BEYOND = DISTANCES.index(1)
+NEAR_FIRST = sorted(range(6), key=lambda pos: abs(DISTANCES[pos]))
 MESH = pl.DeviceIdType.MESH
 F32 = jnp.float32
 BF16 = jnp.bfloat16
@@ -136,8 +137,9 @@
 
     g_copies = [swap(gs, gr, g_ss, g_rs, pos, row_at(d)) for pos, d in enumerate(DISTANCES)]
     x_copies = [swap(xs, xr, x_ss, x_rs, pos, row_at(-d)) for pos, d in enumerate(DISTANCES)]
-    for copy in g_copies + x_copies:
-        copy.start()
+    for copies in (g_copies, x_copies):
+        for pos in reversed(NEAR_FIRST):
+            copies[pos].start()
 
     def three(r):
         start = (r - 1) * BLK
@@ -207,25 +209,27 @@
     first_ref[...] = jnp.zeros_like(first_ref)
     second_ref[...] = jnp.zeros_like(second_ref)
 
-    for copy in x_copies:
-        copy.wait_recv()
-    for pos in range(6):
+    for pos in NEAR_FIRST:
+        x_copies[pos].wait_recv()
         for rank in range(2):
-            s, row, live = read[pos][rank]
-            contrib[2 * pos + rank] = nt(xr[pos, rank], long_ref[s])
-    zacc[0] += nt(xr[BEFORE, 2], band_ref[0, 0])
-    zacc[nb - 1] += nt(xr[BEYOND, 2], band_ref[nb - 1, 2])
-
-    def z_long(r, carry):
-        total = zacc[r]
-        for pos in range(6):
+            contrib[rank] = nt(xr[pos, rank], long_ref[read[pos][rank][0]])
+        if pos == BEFORE:
+            zacc[0] += nt(xr[pos, 2], band_ref[0, 0])
+        if pos == BEYOND:
+            zacc[last] += nt(xr[pos, 2], band_ref[last, 2])
+
+        def z_long(r, carry, pos=pos):
+            total = zacc[r]
             for rank in range(2):
                 s, row, live = read[pos][rank]
-                total += (live * (row == r).astype(F32)) * contrib[2 * pos + rank]
-        z[:, lanes(r)] = total.astype(BF16)
-        return carry
-
-    lax.fori_loop(0, nb, z_long, 0, unroll=2)
+                total += (live * (row == r).astype(F32)) * contrib[rank]
+            if pos == NEAR_FIRST[-1]:
+                z[:, lanes(r)] = total.astype(BF16)
+            else:
+                zacc[r] = total
+            return carry
+
+        lax.fori_loop(0, nb, z_long, 0, unroll=4)
 
     tile = 4 * BLK
     tiles = nodes // tile
@@ -382,7 +386,7 @@
             jax.ShapeDtypeStruct((feats, hidden), F32),
             jax.ShapeDtypeStruct((classes, hidden), F32),
         ),
-        in_specs=[pl.BlockSpec(memory_space=pl.ANY)] * 9,
+        in_specs=[pl.BlockSpec(memory_space=pltpu.HBM)] * 9,
         out_specs=(vmem, vmem, vmem),
         scratch_shapes=[
             pltpu.VMEM(features.shape, BF16),
@@ -420,7 +424,7 @@
             dma((peers,)), dma((peers,)), dma((peers,)), dma((peers,)),
         ],
         compiler_params=pltpu.CompilerParams(
-            collective_id=0, has_side_effects=True, vmem_limit_bytes=40 * 1024 * 1024
+            collective_id=0, has_side_effects=True, vmem_limit_bytes=60 * 1024 * 1024
         ),
     )(features, weight_in, weight_out.T, score_grad, band_blocks, long_blocks, long_rows, long_sources, long_counts)
     second = second.T

time: 42 us -> 36.7 us (0.87)
  local copies, waits for them, and re-layouts: 9.97 us -> 4.61 us
    unnamed x21 -> x3, local copies, waits for them, and re-layouts: 9.97 us -> 4.61 us
where the time goes in v3:
time: 36.7 us; the launch traced here: 36.5 us
  Pallas kernels  31.3 us (85%)
  local copies, waits for them, and re-layouts  4.61 us (13%)
  between operations  0.64 us (2%)
    pallas_call x1, Pallas kernels, local(): pl.pallas_call(functools.partial(kernel, rows_n, cols_n, reduce_here), ou...  31.3 us
    unnamed x3, local copies, waits for them, and re-layouts  4.61 us

profile of v3, /device:TPU:0, one launch (start us, length us, event | category | flops | bytes accessed | tf_op | source)
XLA Modules:
  0.0 36.5 jit_solution(1710708698635357977)
XLA Ops:
  0.6 31.3 %shard_map.112 = (bf16[32,2048]{1,0:T(8,128)(2,1)}, f32[128,256]{1,0:T(8,128)}, f32[64,256]{1,0:T(8,128)}) custom-call(bf16[128,2048]{1,0:T(8,128)(2,1)} %x_hbm.1, bf16[128,256]{1,0:T(8,128)(2,1)} %win_hbm.1, bf16[64,512]{1,0:T(8,128)(2,1)} %bitcast.2, bf16[32,2048]{1,0:T(8,128)(2,1)} %sg_hbm.1, bf16[16,3,128,128]{3,2,1,0:T(8,128)(2,1)} %band_hbm.1, ...), custom_call_target="tpu_custom_call" | custom-call | tf_op jit(solution)/shard_map/pallas_call | solution.py:382
  31.9 1.6 %copy.15 = bf16[32,2048]{1,0:T(8,128)(2,1)} copy(bf16[32,2048]{1,0:T(8,128)(2,1)} %get-tuple-element.12) | data formatting | bytes 262144
  33.5 1.6 %copy.16 = f32[128,256]{1,0:T(8,128)} copy(f32[128,256]{1,0:T(8,128)} %get-tuple-element.13) | data formatting | bytes 262144
  35.0 1.5 %copy.17 = f32[256,64]{0,1:T(8,128)} copy(f32[256,64]{0,1:T(8,128)} %bitcast.3) | data formatting | bytes 131072
